TPU v7x, 32 devices: a whole 2x2x4 slice. The times are simulated.
32 devices in a mesh: rows: 16 (over z, x, core), dirs: 2 (over y).
Axes of the slice: x: 2, y: 2, z: 4, core: 2. Of those that a mesh axis runs over, the one named last changes fastest.
Arguments:
- previous: bfloat16 [24, 32, 128, 512], P('dirs', None, 'rows'), may hold values from -12 to 12
- boundary: float32 [24, 32, 512], P('dirs'), may hold values from -6 to 6
- row_coupling: float32 [24, 128, 512], P('dirs', 'rows'), may hold values from 0 to 1
- cross_gain: float32 [24], P('dirs'), may hold values from 0.5 to 3
- block_inverse: float32 [24, 128, 128], P('dirs'), may hold values from 0 to 1, as said below
- quadrant: int32 [24], P('dirs'), may hold values from 0 to 3
- sea_mask: int32 [128, 512], P('rows'), may hold values from 0 to 1, as said below
- wet_tiles: int32 [128, 4], P('rows'), may hold values 0 or 1
- quad_coef: float32 [32], replicated, may hold values from 0.05 to 0.5
Outputs:
- action: bfloat16 [24, 32, 128, 512], P('dirs', None, 'rows')
Inputs may be any that keep to these rules, and one draw needn't show every extreme that they name: `sea_mask`: in each row the land cells, if any, are the last ones, from a coastline column to the end of the row. block_inverse[d] is the inverse of the 128 x 128 lower bidiagonal matrix with 1 + cross_gain[d] on its diagonal and -cross_gain[d] just below it.
All inputs are finite; a program needn't handle non-finite values. No bound on the sum of `wet_tiles` on one device may be relied on, other than what follows from the above.
Results may differ from a plain program's by a relative error of at most 0.0027.
Values may be sent and summed in bfloat16 or wider, within the bound.
A program may use at most 128 MiB of HBM per device.

v0:
```python
import jax
import jax.numpy as jnp
from jax import lax
from jax.sharding import PartitionSpec as P

SHIFT = 2
highest = lax.Precision.HIGHEST


def compose(preceding_part, following_part):
    return (
        following_part[0] * preceding_part[0],
        following_part[0] * preceding_part[1] + following_part[1],
    )


def higher_band(field):
    return jnp.concatenate([field[:, 1:], jnp.zeros_like(field[:, :1])], axis=1)


def lower_band(field):
    return jnp.concatenate([jnp.zeros_like(field[:, :1]), field[:, :-1]], axis=1)


def quad_terms(center, onward, against, coefficients):
    nonlinear = center * center * (onward + against) - 2.0 * center * onward * against
    return coefficients[None, :, None, None] * nonlinear


def full_source(spectra, coefficients):
    energy = spectra.astype(jnp.float32)
    onward = higher_band(jnp.roll(energy, -SHIFT, axis=0))
    against = lower_band(jnp.roll(energy, SHIFT, axis=0))
    return quad_terms(energy, onward, against, coefficients)


def on_device(
    previous,
    boundary,
    row_coupling,
    cross_gain,
    block_inverse,
    quadrant,
    sea_mask,
    wet_tiles,
    quad_coef,
):
    dir_dev, band_count, row_count, column_count = previous.shape
    block_size = block_inverse.shape[-1]
    sea_cells = sea_mask.astype(jnp.float32)
    backward = quadrant % 2 == 1
    sideways = quadrant // 2 == 1
    couple = row_coupling * sea_cells[None]
    forcing = sea_cells[None, None] * (1.0 - row_coupling)[:, None] * previous.astype(jnp.float32)
    couple = jnp.where(backward[:, None, None], jnp.flip(couple, 1), couple)
    forcing = jnp.where(backward[:, None, None, None], jnp.flip(forcing, 2), forcing)

    def row_step(carry, member):
        gain_now, value_now = carry
        gain_next = member[0][:, None] * gain_now
        value_next = member[0][:, None] * value_now + member[1]
        return ((gain_next, value_next), (gain_next, value_next))

    start_gain = jnp.ones((dir_dev, 1, column_count), jnp.float32)
    start_value = jnp.zeros((dir_dev, band_count, column_count), jnp.float32)
    last_maps, row_maps = lax.scan(
        row_step,
        (start_gain, start_value),
        (jnp.moveaxis(couple, 1, 0), jnp.moveaxis(forcing, 2, 0)),
    )
    span_gain = jnp.moveaxis(row_maps[0], 0, 2)
    partial_value = jnp.moveaxis(row_maps[1], 0, 2)
    block_gain, block_state = last_maps
    every_gain, every_state = (
        lax.all_gather(block_gain[None], "rows", axis=0, tiled=True),
        lax.all_gather(block_state[None], "rows", axis=0, tiled=True),
    )
    device_count = every_gain.shape[0]
    position = lax.axis_index("rows")
    order_flipping = backward[None, :, None, None]
    ordered_gain = jnp.where(order_flipping, jnp.flip(every_gain, 0), every_gain)
    ordered_state = jnp.where(order_flipping, jnp.flip(every_state, 0), every_state)

    def device_step(carry, member):
        return (compose(carry, member), carry)

    _, before_maps = lax.scan(
        device_step,
        (jnp.ones_like(block_gain), jnp.zeros_like(block_state)),
        (ordered_gain, ordered_state),
    )
    before_gain, before_state = before_maps
    onward_gain = lax.dynamic_index_in_dim(before_gain, position, 0, keepdims=False)
    onward_state = lax.dynamic_index_in_dim(before_state, position, 0, keepdims=False)
    against_gain = lax.dynamic_index_in_dim(
        before_gain, device_count - 1 - position, 0, keepdims=False
    )
    against_state = lax.dynamic_index_in_dim(
        before_state, device_count - 1 - position, 0, keepdims=False
    )
    inflow_gain = jnp.where(backward[:, None, None], against_gain, onward_gain)
    inflow_state = jnp.where(backward[:, None, None], against_state, onward_state)
    entering = inflow_gain * boundary + inflow_state
    swept_rows = partial_value + span_gain * entering[:, :, None, :]
    swept_rows = jnp.where(backward[:, None, None, None], jnp.flip(swept_rows, 2), swept_rows)
    flipped = jnp.where(sideways[:, None, None, None], jnp.flip(swept_rows, 3), swept_rows)
    blocks = flipped.reshape(dir_dev, band_count, row_count, column_count // block_size, block_size)
    solved = jnp.einsum(
        "dij,dfrkj->dfrki",
        block_inverse,
        blocks,
        precision=highest,
        preferred_element_type=jnp.float32,
    )
    first_column = block_inverse[:, :, 0][:, None, None, :]
    gain_column = cross_gain[:, None, None, None]
    pieces = [solved[:, :, :, 0]]
    for section in range(1, column_count // block_size):
        pieces.append(solved[:, :, :, section] + gain_column * pieces[-1][..., -1:] * first_column)
    settled = jnp.stack(pieces, 3).reshape(dir_dev, band_count, row_count, column_count)
    settled = (
        jnp.where(sideways[:, None, None, None], jnp.flip(settled, 3), settled)
        * sea_cells[None, None]
    )
    rounded = lax.optimization_barrier(settled.astype(jnp.bfloat16))
    gained = full_source(
        lax.all_to_all(rounded, "dirs", split_axis=2, concat_axis=0, tiled=True), quad_coef
    ).astype(jnp.bfloat16)
    returned = lax.all_to_all(gained, "dirs", split_axis=0, concat_axis=2, tiled=True)
    returned = lax.optimization_barrier(returned)
    wet_cells = jnp.repeat(wet_tiles.astype(jnp.float32), block_size, axis=1)
    return (settled + wet_cells[None, None] * returned.astype(jnp.float32)).astype(jnp.bfloat16)


def solution(mesh):
    in_specs = (
        P("dirs", None, "rows", None),
        P("dirs", None, None),
        P("dirs", "rows", None),
        P("dirs"),
        P("dirs", None, None),
        P("dirs"),
        P("rows", None),
        P("rows", None),
        P(),
    )
    out_specs = P("dirs", None, "rows", None)
    return jax.shard_map(
        on_device, mesh=mesh, in_specs=in_specs, out_specs=out_specs, check_vma=False
    )
```

profile of v0, /device:TPU:0, one launch (start us, length us, event | category | flops | bytes accessed | tf_op | source)
XLA Modules:
  0.0 633.3 jit_solution(5337060883751082020)
XLA Ops:
  14.3 11.2 %rev.27 = f32[12,32,8,512]{3,2,1,0:T(8,128)} reverse(f32[12,32,8,512]{3,2,1,0:T(8,128)} %convert_multiply_fusion), dimensions={2} | reverse | bytes 12582912 | tf_op jit(solution)/shard_map/jit(_flip)/rev | solution.py:56
  33.3 173.7 %while.34 = (s32[]{:T(128)}, f32[12,1,512]{2,1,0:T(1,128)S(1)}, f32[12,32,512]{2,1,0:T(8,128)S(1)}, f32[8,12,1,512]{3,0,1,2:T(8,128)S(1)}, f32[8,12,32,512]{3,0,...) while((s32[]{:T(128)}, f32[12,1,512]{2,1,0:T(1,128)S(1)}, ...), condition=%wide.region_1.2_spmd.clone, body=%wide.region_0.1_spmd.clone.sunk | while | flops 602115 | bytes 7299192 | solution.py:66
  38.3 16.7 %dynamic_update_slice.27 = f32[8,12,32,512]{3,0,2,1:T(8,128)} dynamic-update-slice(f32[8,12,32,512]{3,0,2,1:T(8,128)} %get-tuple-element.342, f32[1,12,32,512]{3,0,2,1:T(1,128)S(1)} %copy.159, s32[]{:T(128)} %get-tuple-element.338, s32[]{:T(128)} %constant.78.clone.1..sunk, s32[]{:T(128)} %constant.78.clone.1..sunk, s32[]{:T(128)} %constant.78.clone.1..sunk) | dynamic-update-slice | bytes 1572868 | tf_op jit(solution)/shard_map/while/body/jit(dynamic_update_index_in_dim)/dynamic_update_slice | solution.py:66
  60.0 16.7 %dynamic_update_slice.27 = f32[8,12,32,512]{3,0,2,1:T(8,128)} dynamic-update-slice(f32[8,12,32,512]{3,0,2,1:T(8,128)} %get-tuple-element.342, f32[1,12,32,512]{3,0,2,1:T(1,128)S(1)} %copy.159, s32[]{:T(128)} %get-tuple-element.338, s32[]{:T(128)} %constant.78.clone.1..sunk, s32[]{:T(128)} %constant.78.clone.1..sunk, s32[]{:T(128)} %constant.78.clone.1..sunk) | dynamic-update-slice | bytes 1572868 | tf_op jit(solution)/shard_map/while/body/jit(dynamic_update_index_in_dim)/dynamic_update_slice | solution.py:66
  81.7 16.7 %dynamic_update_slice.27 = f32[8,12,32,512]{3,0,2,1:T(8,128)} dynamic-update-slice(f32[8,12,32,512]{3,0,2,1:T(8,128)} %get-tuple-element.342, f32[1,12,32,512]{3,0,2,1:T(1,128)S(1)} %copy.159, s32[]{:T(128)} %get-tuple-element.338, s32[]{:T(128)} %constant.78.clone.1..sunk, s32[]{:T(128)} %constant.78.clone.1..sunk, s32[]{:T(128)} %constant.78.clone.1..sunk) | dynamic-update-slice | bytes 1572868 | tf_op jit(solution)/shard_map/while/body/jit(dynamic_update_index_in_dim)/dynamic_update_slice | solution.py:66
  103.4 16.7 %dynamic_update_slice.27 = f32[8,12,32,512]{3,0,2,1:T(8,128)} dynamic-update-slice(f32[8,12,32,512]{3,0,2,1:T(8,128)} %get-tuple-element.342, f32[1,12,32,512]{3,0,2,1:T(1,128)S(1)} %copy.159, s32[]{:T(128)} %get-tuple-element.338, s32[]{:T(128)} %constant.78.clone.1..sunk, s32[]{:T(128)} %constant.78.clone.1..sunk, s32[]{:T(128)} %constant.78.clone.1..sunk) | dynamic-update-slice | bytes 1572868 | tf_op jit(solution)/shard_map/while/body/jit(dynamic_update_index_in_dim)/dynamic_update_slice | solution.py:66
  125.1 16.7 %dynamic_update_slice.27 = f32[8,12,32,512]{3,0,2,1:T(8,128)} dynamic-update-slice(f32[8,12,32,512]{3,0,2,1:T(8,128)} %get-tuple-element.342, f32[1,12,32,512]{3,0,2,1:T(1,128)S(1)} %copy.159, s32[]{:T(128)} %get-tuple-element.338, s32[]{:T(128)} %constant.78.clone.1..sunk, s32[]{:T(128)} %constant.78.clone.1..sunk, s32[]{:T(128)} %constant.78.clone.1..sunk) | dynamic-update-slice | bytes 1572868 | tf_op jit(solution)/shard_map/while/body/jit(dynamic_update_index_in_dim)/dynamic_update_slice | solution.py:66
  146.8 16.7 %dynamic_update_slice.27 = f32[8,12,32,512]{3,0,2,1:T(8,128)} dynamic-update-slice(f32[8,12,32,512]{3,0,2,1:T(8,128)} %get-tuple-element.342, f32[1,12,32,512]{3,0,2,1:T(1,128)S(1)} %copy.159, s32[]{:T(128)} %get-tuple-element.338, s32[]{:T(128)} %constant.78.clone.1..sunk, s32[]{:T(128)} %constant.78.clone.1..sunk, s32[]{:T(128)} %constant.78.clone.1..sunk) | dynamic-update-slice | bytes 1572868 | tf_op jit(solution)/shard_map/while/body/jit(dynamic_update_index_in_dim)/dynamic_update_slice | solution.py:66
  168.5 16.7 %dynamic_update_slice.27 = f32[8,12,32,512]{3,0,2,1:T(8,128)} dynamic-update-slice(f32[8,12,32,512]{3,0,2,1:T(8,128)} %get-tuple-element.342, f32[1,12,32,512]{3,0,2,1:T(1,128)S(1)} %copy.159, s32[]{:T(128)} %get-tuple-element.338, s32[]{:T(128)} %constant.78.clone.1..sunk, s32[]{:T(128)} %constant.78.clone.1..sunk, s32[]{:T(128)} %constant.78.clone.1..sunk) | dynamic-update-slice | bytes 1572868 | tf_op jit(solution)/shard_map/while/body/jit(dynamic_update_index_in_dim)/dynamic_update_slice | solution.py:66
  190.3 16.7 %dynamic_update_slice.27 = f32[8,12,32,512]{3,0,2,1:T(8,128)} dynamic-update-slice(f32[8,12,32,512]{3,0,2,1:T(8,128)} %get-tuple-element.342, f32[1,12,32,512]{3,0,2,1:T(1,128)S(1)} %copy.159, s32[]{:T(128)} %get-tuple-element.338, s32[]{:T(128)} %constant.78.clone.1..sunk, s32[]{:T(128)} %constant.78.clone.1..sunk, s32[]{:T(128)} %constant.78.clone.1..sunk) | dynamic-update-slice | bytes 1572868 | tf_op jit(solution)/shard_map/while/body/jit(dynamic_update_index_in_dim)/dynamic_update_slice | solution.py:66
  208.4 25.4 %all-gather = f32[192,1,512]{2,1,0:T(1,128)S(1)} all-gather(f32[12,1,512]{2,1,0:T(1,128)S(1)} %get-tuple-element.85), channel_id=2, replica_groups=mesh['rows'=16,'dirs'=2] {'rows'}, dimensions={0}, use_global_device_ids=true | all-gather | bytes 417792 | tf_op jit(solution)/shard_map/all_gather | solution.py:75
  234.9 77.5 %all-gather.4.cloned.1.call-done = f32[192,32,512]{2,1,0:T(8,128)} async-done(((f32[12,32,512]{2,1,0:T(8,128)}), f32[192,32,512]{2,1,0:T(8,128)}) %all-gather.4.cloned.1.call-update) | async-done | bytes 12582928 | tf_op jit(solution)/shard_map/all_gather | solution.py:76
  312.4 17.5 %reverse_select_fusion = f32[16,12,32,512]{3,2,1,0:T(8,128)} fusion(f32[16,12,32,512]{3,2,1,0:T(8,128)} %bitcast.110, pred[12]{0:T(512)(128)(4,1)S(1)} %get-tuple-element.234), kind=kLoop, calls=%fused_computation.15 | loop fusion | flops 3145728 | bytes 25165836 | tf_op jit(solution)/shard_map/jit(_where)/select_n | solution.py:82
  329.9 61.8 %while.35 = (s32[]{:T(128)}, f32[12,1,512]{2,1,0:T(1,128)S(1)}, f32[12,32,512]{2,1,0:T(8,128)S(1)}, f32[16,12,1,512]{3,2,1,0:T(1,128)}, f32[16,12,32,512]{3,2,1,...) while((s32[]{:T(128)}, f32[12,1,512]{2,1,0:T(1,128)S(1)}, ...), condition=%wide.region_3.4_spmd.clone, body=%wide.region_2.3_spmd.clone.sunk | while | flops 804867 | bytes 4154482 | solution.py:87
  400.8 11.2 %rev.30 = f32[12,32,8,512]{3,2,1,0:T(8,128)} reverse(f32[12,32,8,512]{3,2,1,0:T(8,128)} %bitcast_add_fusion.1), dimensions={2} | reverse | bytes 12582912 | tf_op jit(solution)/shard_map/jit(_flip)/rev | solution.py:105
  412.0 9.4 %broadcast_select_fusion.2 = f32[12,32,8,512]{3,2,1,0:T(8,128)} fusion(f32[12,32,8,512]{3,2,1,0:T(8,128)} %rev.30, pred[12]{0:T(512)(128)(4,1)S(1)} %get-tuple-element.234, f32[12,32,512]{2,1,0:T(8,128)S(1)} %fusion.8, f32[12,8,512]{2,1,0:T(8,128)S(1)} %bitcast.119, f32[8,12,32,512]{3,0,2,1:T(8,128)} %get-tuple-element.83), kind=kLoop, calls=%fused_computation.34 | loop fusion | flops 4718592 | bytes 19857420 | tf_op jit(solution)/shard_map/jit(_where)/select_n | solution.py:105
  421.5 12.5 %rev.31 = f32[12,32,8,512]{3,2,1,0:T(8,128)} reverse(f32[12,32,8,512]{3,2,1,0:T(8,128)} %broadcast_select_fusion.2), dimensions={3} | reverse | bytes 12582912 | tf_op jit(solution)/shard_map/jit(_flip)/rev | solution.py:106
  433.9 8.6 %fusion.2 = f32[12,32,8,4,128]{4,2,3,1,0:T(8,128)S(1)} fusion(f32[12,32,8,512]{3,2,1,0:T(8,128)} %rev.31, f32[12,32,8,512]{3,2,1,0:T(8,128)} %broadcast_select_fusion.2, pred[12]{0:T(512)(128)(4,1)S(1)} %get-tuple-element.233, f32[12,128,128]{2,1,0:T(8,128)S(1)} %copy-done.1), kind=kOutput, calls=%fused_computation.22 | convolution fusion | flops 2417491968 | bytes 19660812 | tf_op jit(solution)/shard_map/dij,dfrkj->dfrki/dot_general | solution.py:108
  466.7 14.3 %multiply_add_fusion.2 = (f32[12,32,8,1,128]{1,2,4,0,3:T(8,128)}, f32[12,32,8,1,128]{1,2,4,0,3:T(8,128)}, f32[12,32,8,1,128]{1,2,4,0,3:T(8,128)}) fusion(f32[12,32,8,1,128]{1,2,4,0,3:T(8,128)} %copy.137, f32[12,128]{1,0:T(8,128)S(1)} %bitcast.121, f32[12,32,8]{1,2,0:T(8,128)S(1)} %fusion.13, f32[12,32,8,1,128]{1,2,4,0,3:T(8,128)} %copy.139, ...), kind=kLoop, calls=%fused_computation.30 | loop fusion | flops 2359296 | bytes 9480192 | tf_op jit(solution)/shard_map/add | solution.py:119
  502.0 12.5 %rev.32 = f32[12,32,8,512]{3,2,1,0:T(8,128)} reverse(f32[12,32,8,512]{3,2,1,0:T(8,128)} %maximum_bitcast_fusion), dimensions={3} | reverse | bytes 12582912 | tf_op jit(solution)/shard_map/jit(_flip)/rev | solution.py:122
  520.3 39.4 %all_to_all.27 = bf16[12,32,8,512]{3,1,0,2:T(8,128)(2,1)S(1)} all-to-all(bf16[12,32,8,512]{3,1,0,2:T(8,128)(2,1)S(1)} %copy.121), channel_id=1, replica_groups=mesh['rows'=16,'dirs'=2] {'dirs'}, dimensions={2} | all-to-all | bytes 6291456 | tf_op jit(solution)/shard_map/all_to_all | solution.py:127
  567.7 7.7 %multiply_convert_fusion = bf16[24,32,4,512]{3,1,2,0:T(8,128)(2,1)} fusion(f32[2,32,4,512]{3,1,2,0:T(8,128)S(1)} %get-tuple-element.219, f32[22,32,4,512]{3,1,2,0:T(8,128)} %get-tuple-element.221, f32[22,32,4,512]{3,1,2,0:T(8,128)} %get-tuple-element.220, f32[2,32,4,512]{3,1,2,0:T(8,128)S(1)} %get-tuple-element.218, f32[32]{0:T(128)S(1)} %copy-done.5, ...), kind=kLoop, calls=%fused_computation.26 | loop fusion | flops 26738688 | bytes 22020224 | tf_op jit(solution)/shard_map/convert_element_type | solution.py:128
  580.8 35.9 %all-to-all-done.1 = bf16[24,32,4,512]{3,1,2,0:T(8,128)(2,1)} async-done(((bf16[24,32,4,512]{3,1,2,0:T(8,128)(2,1)}), bf16[24,32,4,512]{3,1,2,0:T(8,128)(2,1)}, u32[]{:S(2)}, u32[]{:S(2)}) %all-to-all-start.1) | async-done | bytes 3145760 | tf_op jit(solution)/shard_map/all_to_all | solution.py:129
  618.8 7.6 %add_convert_fusion = bf16[12,32,8,512]{3,2,1,0:T(8,128)(2,1)} fusion(bf16[12,32,8,512]{3,1,2,0:T(8,128)(2,1)S(1)} %bitcast.111, f32[8,512]{1,0:T(8,128)S(1)} %broadcast_bitcast_fusion, f32[8,512]{1,0:T(8,128)S(1)} %convert_element_type.33, f32[12,32,8,512]{3,2,1,0:T(8,128)} %rev.32, pred[12]{0:T(512)(128)(4,1)S(1)} %get-tuple-element.233, ...), kind=kLoop, calls=%fused_computation.25 | loop fusion | flops 14155776 | bytes 18907148 | tf_op jit(solution)/shard_map/convert_element_type | solution.py:132
  (187 shorter events, 194.9 us)
Async XLA Ops:
  6.5 305.9 %all-gather.4.cloned.1.call-start = ((), (), s32[]{:S(2)}) async-start(), calls=%async_computation.2 | async-start | bytes 13369344 | tf_op jit(solution)/shard_map/all_gather | solution.py:76
  33.3 174.7 %copy-start.1 = (f32[12,128,128]{2,1,0:T(8,128)S(1)}, f32[12,128,128]{2,1,0:T(8,128)}, u32[]{:S(2)}) copy-start(f32[12,128,128]{2,1,0:T(8,128)} %param.17) | copy-start | bytes 2359300
  207.1 0.9 copy-start
  329.9 62.6 %copy-start.2 = (f32[12,32,512]{2,1,0:T(8,128)S(1)}, f32[12,32,512]{2,1,0:T(8,128)}, u32[]{:S(2)}) copy-start(f32[12,32,512]{2,1,0:T(8,128)} %param.14) | copy-start | bytes 2359300
  454.0 10.1 %copy-start.3 = (f32[12]{0:T(128)S(1)}, f32[12]{0:T(128)}, u32[]{:S(2)}) copy-start(f32[12]{0:T(128)} %param.16) | copy-start | bytes 148
  561.8 5.8 copy-start.5
  575.3 5.3 copy-start.4
  575.3 41.4 %all-to-all-start.1 = ((bf16[24,32,4,512]{3,1,2,0:T(8,128)(2,1)}), bf16[24,32,4,512]{3,1,2,0:T(8,128)(2,1)}, u32[]{:S(2)}, u32[]{:S(2)}) async-start(bf16[24,32,4,512]{3,1,2,0:T(8,128)(2,1)} %multiply_convert_fusion), calls=%async_computation.1 | async-start | bytes 6291456 | tf_op jit(solution)/shard_map/all_to_all | solution.py:129
Sparse Core Ops, SparseCore 0:
  208.1 104.2 all-gather.3
where the time goes:
time: 641 us; the launch traced here: 633 us
  local copies, waits for them, and re-layouts  268 us (42%)
  other arithmetic  159 us (25%)
  waiting for transfers between devices  113 us (18%)
  blocking collectives  64.8 us (10%)
  between operations  13.6 us (2%)
  matrix products  8.55 us (1%)
    dynamic_update_slice x24, local copies, waits for them, and re-layouts, on_device(): lax.scan(row_step, (start_gain, start_value), (jnp.moveaxis(couple, 1, 0)...  141 us
    all_gather x1, waiting for transfers between devices, on_device(): lax.all_gather(block_state[None], 'rows', axis=0, tiled=True)  77.5 us
    all_to_all x1, blocking collectives, on_device(): lax.all_to_all(rounded, 'dirs', split_axis=2, concat_axis=0, tiled=True)  39.4 us
    all_to_all x1, waiting for transfers between devices, on_device(): lax.all_to_all(gained, 'dirs', split_axis=0, concat_axis=2, tiled=True)  35.9 us
    dynamic_slice x8, local copies, waits for them, and re-layouts, on_device(): lax.scan(row_step, (start_gain, start_value), (jnp.moveaxis(couple, 1, 0)...  29 us
    dynamic_update_slice x32, other arithmetic, on_device(): lax.scan(device_step, (jnp.ones_like(block_gain), jnp.zeros_like(block_st...  25.5 us
    all_gather x1, blocking collectives, on_device(): lax.all_gather(block_gain[None], 'rows', axis=0, tiled=True)  25.4 us
    add x16, other arithmetic, compose(): following_part[0] * preceding_part[1] + following_part[1]  23.1 us
  transfers between devices with their start and end apart: 2, of which 2 were waited for; matrix products, arithmetic and copies ran while one was open for 0% of the time, Pallas kernels for 0%

commit v1 on v0

--- a/solution.py
+++ b/solution.py
@@ -5,6 +5,29 @@
 
 SHIFT = 2
 highest = lax.Precision.HIGHEST
+
+
+def build_forms_all(in_array, chip_axis):
+    field_out, f_next, reached = (
+        jax.lax.axis_size(chip_axis),
+        jax.lax.axis_index(chip_axis),
+        in_array.shape[0],
+    )
+    r1, opened = (in_array, 1)
+    while opened < field_out:
+        r1 = jnp.concatenate(
+            [
+                r1,
+                jax.lax.ppermute(
+                    r1,
+                    chip_axis,
+                    tuple(((dev, (dev - opened) % field_out) for dev in range(field_out))),
+                ),
+            ],
+            axis=0,
+        )
+        opened = 2 * opened
+    return jnp.roll(r1, f_next * reached, axis=0)
 
 
 def compose(preceding_part, following_part):
@@ -73,7 +96,7 @@
     block_gain, block_state = last_maps
     every_gain, every_state = (
         lax.all_gather(block_gain[None], "rows", axis=0, tiled=True),
-        lax.all_gather(block_state[None], "rows", axis=0, tiled=True),
+        build_forms_all(block_state[None], "rows"),
     )
     device_count = every_gain.shape[0]
     position = lax.axis_index("rows")

time: 641 us -> 966 us (1.51)
  blocking collectives: 64.8 us -> 318 us
  local copies, waits for them, and re-layouts: 268 us -> 306 us
  waiting for transfers between devices: 113 us -> 150 us
  between operations: 13.6 us -> 0.23 us
    all_gather x1, blocking collectives: 25.4 us -> 278 us  [on_device(): lax.all_gather(block_gain[None], 'rows', axis=0, tiled=True)]
    ppermute x0 -> x4, waiting for transfers between devices: none -> 114 us  [build_forms_all(): jax.lax.ppermute(r1, chip_axis, tuple(((dev, (dev - opened) % field_out)...]
    all_gather x1 -> x0, waiting for transfers between devices: 77.5 us -> none  [on_device(): lax.all_gather(block_state[None], 'rows', axis=0, tiled=True)]
    unnamed x17 -> x36, local copies, waits for them, and re-layouts: 20.3 us -> 40.1 us
    dynamic_slice x0 -> x1, local copies, waits for them, and re-layouts: none -> 12 us  [build_forms_all(): return jnp.roll(r1, f_next * reached, axis=0)]
  transfers between devices with their start and end apart: 2 -> 5, of which waited for: 2 -> 4; matrix products, arithmetic and copies ran while one was open for 0% -> 1% of each run, Pallas kernels for 0% -> 0%
where the time goes in v1:
time: 966 us; the launch traced here: 958 us
  blocking collectives  318 us (33%)
  local copies, waits for them, and re-layouts  306 us (32%)
  other arithmetic  162 us (17%)
  waiting for transfers between devices  150 us (16%)
  starting transfers between devices  13 us (1%)
    all_gather x1, blocking collectives, on_device(): lax.all_gather(block_gain[None], 'rows', axis=0, tiled=True)  278 us
    dynamic_update_slice x24, local copies, waits for them, and re-layouts, on_device(): lax.scan(row_step, (start_gain, start_value), (jnp.moveaxis(couple, 1, 0)...  141 us
    ppermute x4, waiting for transfers between devices, build_forms_all(): jax.lax.ppermute(r1, chip_axis, tuple(((dev, (dev - opened) % field_out)...  114 us
    unnamed x36, local copies, waits for them, and re-layouts  40.1 us
    all_to_all x1, blocking collectives, on_device(): lax.all_to_all(rounded, 'dirs', split_axis=2, concat_axis=0, tiled=True)  39.5 us
    all_to_all x1, waiting for transfers between devices, on_device(): lax.all_to_all(gained, 'dirs', split_axis=0, concat_axis=2, tiled=True)  36 us
    dynamic_slice x8, local copies, waits for them, and re-layouts, on_device(): lax.scan(row_step, (start_gain, start_value), (jnp.moveaxis(couple, 1, 0)...  28.9 us
    dynamic_update_slice x32, other arithmetic, on_device(): lax.scan(device_step, (jnp.ones_like(block_gain), jnp.zeros_like(block_st...  26.2 us
  transfers between devices with their start and end apart: 5, of which 4 were waited for; matrix products, arithmetic and copies ran while one was open for 1% of the time, Pallas kernels for 0%

profile of v1, /device:TPU:0, one launch (start us, length us, event | category | flops | bytes accessed | tf_op | source)
XLA Modules:
  0.0 958.0 jit_solution(5099604568214628415)
XLA Ops:
  7.8 11.2 %rev.27 = f32[12,32,8,512]{3,2,1,0:T(8,128)} reverse(f32[12,32,8,512]{3,2,1,0:T(8,128)} %convert_multiply_fusion), dimensions={2} | reverse | bytes 12582912 | tf_op jit(solution)/shard_map/jit(_flip)/rev | solution.py:79
  26.8 174.0 %while.34 = (s32[]{:T(128)}, f32[12,1,512]{2,1,0:T(1,128)S(1)}, f32[12,32,512]{2,1,0:T(8,128)S(1)}, f32[8,12,1,512]{3,0,1,2:T(8,128)S(1)}, f32[8,12,32,512]{3,0,...) while((s32[]{:T(128)}, f32[12,1,512]{2,1,0:T(1,128)S(1)}, ...), condition=%wide.region_1.2_spmd.clone, body=%wide.region_0.1_spmd.clone.sunk | while | flops 602115 | bytes 7299192 | solution.py:89
  31.7 16.7 %dynamic_update_slice.27 = f32[8,12,32,512]{3,0,2,1:T(8,128)} dynamic-update-slice(f32[8,12,32,512]{3,0,2,1:T(8,128)} %get-tuple-element.342, f32[1,12,32,512]{3,0,2,1:T(1,128)S(1)} %copy.159, s32[]{:T(128)} %get-tuple-element.338, s32[]{:T(128)} %constant.96.clone.1..sunk, s32[]{:T(128)} %constant.96.clone.1..sunk, s32[]{:T(128)} %constant.96.clone.1..sunk) | dynamic-update-slice | bytes 1572868 | tf_op jit(solution)/shard_map/while/body/jit(dynamic_update_index_in_dim)/dynamic_update_slice | solution.py:89
  53.5 16.7 %dynamic_update_slice.27 = f32[8,12,32,512]{3,0,2,1:T(8,128)} dynamic-update-slice(f32[8,12,32,512]{3,0,2,1:T(8,128)} %get-tuple-element.342, f32[1,12,32,512]{3,0,2,1:T(1,128)S(1)} %copy.159, s32[]{:T(128)} %get-tuple-element.338, s32[]{:T(128)} %constant.96.clone.1..sunk, s32[]{:T(128)} %constant.96.clone.1..sunk, s32[]{:T(128)} %constant.96.clone.1..sunk) | dynamic-update-slice | bytes 1572868 | tf_op jit(solution)/shard_map/while/body/jit(dynamic_update_index_in_dim)/dynamic_update_slice | solution.py:89
  75.2 16.7 %dynamic_update_slice.27 = f32[8,12,32,512]{3,0,2,1:T(8,128)} dynamic-update-slice(f32[8,12,32,512]{3,0,2,1:T(8,128)} %get-tuple-element.342, f32[1,12,32,512]{3,0,2,1:T(1,128)S(1)} %copy.159, s32[]{:T(128)} %get-tuple-element.338, s32[]{:T(128)} %constant.96.clone.1..sunk, s32[]{:T(128)} %constant.96.clone.1..sunk, s32[]{:T(128)} %constant.96.clone.1..sunk) | dynamic-update-slice | bytes 1572868 | tf_op jit(solution)/shard_map/while/body/jit(dynamic_update_index_in_dim)/dynamic_update_slice | solution.py:89
  97.0 16.7 %dynamic_update_slice.27 = f32[8,12,32,512]{3,0,2,1:T(8,128)} dynamic-update-slice(f32[8,12,32,512]{3,0,2,1:T(8,128)} %get-tuple-element.342, f32[1,12,32,512]{3,0,2,1:T(1,128)S(1)} %copy.159, s32[]{:T(128)} %get-tuple-element.338, s32[]{:T(128)} %constant.96.clone.1..sunk, s32[]{:T(128)} %constant.96.clone.1..sunk, s32[]{:T(128)} %constant.96.clone.1..sunk) | dynamic-update-slice | bytes 1572868 | tf_op jit(solution)/shard_map/while/body/jit(dynamic_update_index_in_dim)/dynamic_update_slice | solution.py:89
  118.7 16.7 %dynamic_update_slice.27 = f32[8,12,32,512]{3,0,2,1:T(8,128)} dynamic-update-slice(f32[8,12,32,512]{3,0,2,1:T(8,128)} %get-tuple-element.342, f32[1,12,32,512]{3,0,2,1:T(1,128)S(1)} %copy.159, s32[]{:T(128)} %get-tuple-element.338, s32[]{:T(128)} %constant.96.clone.1..sunk, s32[]{:T(128)} %constant.96.clone.1..sunk, s32[]{:T(128)} %constant.96.clone.1..sunk) | dynamic-update-slice | bytes 1572868 | tf_op jit(solution)/shard_map/while/body/jit(dynamic_update_index_in_dim)/dynamic_update_slice | solution.py:89
  140.4 16.7 %dynamic_update_slice.27 = f32[8,12,32,512]{3,0,2,1:T(8,128)} dynamic-update-slice(f32[8,12,32,512]{3,0,2,1:T(8,128)} %get-tuple-element.342, f32[1,12,32,512]{3,0,2,1:T(1,128)S(1)} %copy.159, s32[]{:T(128)} %get-tuple-element.338, s32[]{:T(128)} %constant.96.clone.1..sunk, s32[]{:T(128)} %constant.96.clone.1..sunk, s32[]{:T(128)} %constant.96.clone.1..sunk) | dynamic-update-slice | bytes 1572868 | tf_op jit(solution)/shard_map/while/body/jit(dynamic_update_index_in_dim)/dynamic_update_slice | solution.py:89
  162.2 16.7 %dynamic_update_slice.27 = f32[8,12,32,512]{3,0,2,1:T(8,128)} dynamic-update-slice(f32[8,12,32,512]{3,0,2,1:T(8,128)} %get-tuple-element.342, f32[1,12,32,512]{3,0,2,1:T(1,128)S(1)} %copy.159, s32[]{:T(128)} %get-tuple-element.338, s32[]{:T(128)} %constant.96.clone.1..sunk, s32[]{:T(128)} %constant.96.clone.1..sunk, s32[]{:T(128)} %constant.96.clone.1..sunk) | dynamic-update-slice | bytes 1572868 | tf_op jit(solution)/shard_map/while/body/jit(dynamic_update_index_in_dim)/dynamic_update_slice | solution.py:89
  183.9 16.7 %dynamic_update_slice.27 = f32[8,12,32,512]{3,0,2,1:T(8,128)} dynamic-update-slice(f32[8,12,32,512]{3,0,2,1:T(8,128)} %get-tuple-element.342, f32[1,12,32,512]{3,0,2,1:T(1,128)S(1)} %copy.159, s32[]{:T(128)} %get-tuple-element.338, s32[]{:T(128)} %constant.96.clone.1..sunk, s32[]{:T(128)} %constant.96.clone.1..sunk, s32[]{:T(128)} %constant.96.clone.1..sunk) | dynamic-update-slice | bytes 1572868 | tf_op jit(solution)/shard_map/while/body/jit(dynamic_update_index_in_dim)/dynamic_update_slice | solution.py:89
  206.3 9.5 collective-permute-done
  216.6 34.2 %collective-permute-done.1 = f32[2,12,32,512]{3,2,1,0:T(8,128)S(1)} collective-permute-done((f32[2,12,32,512]{3,2,1,0:T(8,128)S(1)}, f32[2,12,32,512]{3,2,1,0:T(8,128)S(1)}, u32[]{:S(2)}, u32[]{:S(2)}) %collective-permute-start.1) | collective-permute-done | bytes 1572896 | tf_op jit(solution)/shard_map/ppermute | solution.py:21
  251.8 70.2 %collective-permute-done.2 = f32[4,12,32,512]{3,2,1,0:T(8,128)S(1)} collective-permute-done((f32[4,12,32,512]{3,2,1,0:T(8,128)S(1)}, f32[4,12,32,512]{3,2,1,0:T(8,128)S(1)}, u32[]{:S(2)}, u32[]{:S(2)}) %collective-permute-start.2) | collective-permute-done | bytes 3145760 | tf_op jit(solution)/shard_map/ppermute | solution.py:21
  329.3 278.3 %all-gather = f32[192,1,512]{2,1,0:T(1,128)S(1)} all-gather(f32[12,1,512]{2,1,0:T(1,128)S(1)} %get-tuple-element.85), channel_id=2, replica_groups=mesh['rows'=16,'dirs'=2] {'rows'}, dimensions={0}, use_global_device_ids=true | all-gather | bytes 417792 | tf_op jit(solution)/shard_map/all_gather | solution.py:98
  633.9 12.0 %constant_dynamic-slice_fusion.5 = f32[16,12,32,512]{3,2,1,0:T(8,128)} fusion(f32[32,12,32,512]{3,2,1,0:T(8,128)} %constant_dynamic-update-slice_fusion, s32[]{:T(128)S(6)} %select_n.78), kind=kLoop, calls=%fused_computation.71 | loop fusion | bytes 25165828 | tf_op jit(solution)/shard_map/jit(_roll_dynamic)/dynamic_slice | solution.py:30
  645.9 17.5 %reverse_select_fusion = f32[16,12,32,512]{3,2,1,0:T(8,128)} fusion(f32[16,12,32,512]{3,2,1,0:T(8,128)} %constant_dynamic-slice_fusion.5, pred[12]{0:T(512)(128)(4,1)S(1)} %get-tuple-element.234), kind=kLoop, calls=%fused_computation.15 | loop fusion | flops 3145728 | bytes 25165836 | tf_op jit(solution)/shard_map/jit(_where)/select_n | solution.py:105
  663.4 62.5 %while.35 = (s32[]{:T(128)}, f32[12,1,512]{2,1,0:T(1,128)S(1)}, f32[12,32,512]{2,1,0:T(8,128)S(1)}, f32[16,12,1,512]{3,2,1,0:T(1,128)}, f32[16,12,32,512]{3,2,1,...) while((s32[]{:T(128)}, f32[12,1,512]{2,1,0:T(1,128)S(1)}, ...), condition=%wide.region_3.4_spmd.clone, body=%wide.region_2.3_spmd.clone.sunk | while | flops 804867 | bytes 4154482 | solution.py:110
  735.0 11.2 %rev.30 = f32[12,32,8,512]{3,2,1,0:T(8,128)} reverse(f32[12,32,8,512]{3,2,1,0:T(8,128)} %bitcast_add_fusion.1), dimensions={2} | reverse | bytes 12582912 | tf_op jit(solution)/shard_map/jit(_flip)/rev | solution.py:128
  746.2 9.4 broadcast_select_fusion.2
  755.6 12.5 %rev.31 = f32[12,32,8,512]{3,2,1,0:T(8,128)} reverse(f32[12,32,8,512]{3,2,1,0:T(8,128)} %broadcast_select_fusion.2), dimensions={3} | reverse | bytes 12582912 | tf_op jit(solution)/shard_map/jit(_flip)/rev | solution.py:129
  799.9 14.4 %multiply_add_fusion.2 = (f32[12,32,8,1,128]{1,2,4,0,3:T(8,128)}, f32[12,32,8,1,128]{1,2,4,0,3:T(8,128)}, f32[12,32,8,1,128]{1,2,4,0,3:T(8,128)}) fusion(f32[12,32,8,1,128]{1,2,4,0,3:T(8,128)} %copy.137, f32[12,128]{1,0:T(8,128)S(1)} %bitcast.126, f32[12,32,8]{1,2,0:T(8,128)S(1)} %fusion.13, f32[12,32,8,1,128]{1,2,4,0,3:T(8,128)} %copy.139, ...), kind=kLoop, calls=%fused_computation.31 | loop fusion | flops 2359296 | bytes 9480192 | tf_op jit(solution)/shard_map/add | solution.py:142
  834.0 12.4 %rev.32 = f32[12,32,8,512]{3,2,1,0:T(8,128)} reverse(f32[12,32,8,512]{3,2,1,0:T(8,128)} %maximum_bitcast_fusion), dimensions={3} | reverse | bytes 12582912 | tf_op jit(solution)/shard_map/jit(_flip)/rev | solution.py:145
  851.8 39.5 %all_to_all.27 = bf16[12,32,8,512]{3,1,0,2:T(8,128)(2,1)S(1)} all-to-all(bf16[12,32,8,512]{3,1,0,2:T(8,128)(2,1)S(1)} %copy.121), channel_id=1, replica_groups=mesh['rows'=16,'dirs'=2] {'dirs'}, dimensions={2} | all-to-all | bytes 6291456 | tf_op jit(solution)/shard_map/all_to_all | solution.py:150
  912.3 36.0 %all-to-all-done.1 = bf16[24,32,4,512]{3,1,2,0:T(8,128)(2,1)} async-done(((bf16[24,32,4,512]{3,1,2,0:T(8,128)(2,1)}), bf16[24,32,4,512]{3,1,2,0:T(8,128)(2,1)}, u32[]{:S(2)}, u32[]{:S(2)}) %all-to-all-start.1) | async-done | bytes 3145760 | tf_op jit(solution)/shard_map/all_to_all | solution.py:152
  (216 shorter events, 255.0 us)
Async XLA Ops:
  200.8 15.0 %collective-permute-start = (f32[1,12,32,512]{3,2,1,0:T(8,128)S(1)}, f32[1,12,32,512]{3,2,1,0:T(8,128)S(1)}, u32[]{:S(2)}, u32[]{:S(2)}) collective-permute-start(f32[1,12,32,512]{3,2,1,0:T(8,128)S(1)} %bitcast.107), channel_id=1, source_target_pairs={{0,30},{2,0},{4,2},{6,4},{8,6},{10,8},{12,10},{14,12},{16,14},{18,... | collective-permute-start | bytes 2359304 | tf_op jit(solution)/shard_map/ppermute | solution.py:21
  215.8 111.0 %copy-start.4 = (f32[1,12,32,512]{3,2,1,0:T(8,128)}, f32[1,12,32,512]{3,2,1,0:T(8,128)S(1)}, u32[]{:S(2)}) copy-start(f32[1,12,32,512]{3,2,1,0:T(8,128)S(1)} %collective-permute-done) | copy-start | bytes 2359300
  216.0 34.8 %collective-permute-start.1 = (f32[2,12,32,512]{3,2,1,0:T(8,128)S(1)}, f32[2,12,32,512]{3,2,1,0:T(8,128)S(1)}, u32[]{:S(2)}, u32[]{:S(2)}) collective-permute-start(f32[2,12,32,512]{3,2,1,0:T(8,128)S(1)} %pad_maximum_fusion.2), channel_id=1, source_target_pairs={{0,28},{2,30},{4,0},{6,2},{8,4},{10,6},{12,8},{14,10},{16,12},{18,... | collective-permute-start | bytes 4718600 | tf_op jit(solution)/shard_map/ppermute | solution.py:21
  251.3 70.8 %collective-permute-start.2 = (f32[4,12,32,512]{3,2,1,0:T(8,128)S(1)}, f32[4,12,32,512]{3,2,1,0:T(8,128)S(1)}, u32[]{:S(2)}, u32[]{:S(2)}) collective-permute-start(f32[4,12,32,512]{3,2,1,0:T(8,128)S(1)} %pad_maximum_fusion.1), channel_id=1, source_target_pairs={{0,24},{2,26},{4,28},{6,30},{8,0},{10,2},{12,4},{14,6},{16,8},{18,... | collective-permute-start | bytes 9437192 | tf_op jit(solution)/shard_map/ppermute | solution.py:21
  322.1 1.7 copy-start
  326.7 288.3 %collective-permute-start.3 = (f32[8,12,32,512]{3,2,1,0:T(8,128)}, f32[8,12,32,512]{3,2,1,0:T(8,128)}, u32[]{:S(2)}, u32[]{:S(2)}) collective-permute-start(f32[8,12,32,512]{3,2,1,0:T(8,128)} %pad_maximum_fusion), channel_id=1, source_target_pairs={{0,16},{2,18},{4,20},{6,22},{8,24},{10,26},{12,28},{14,30},{16,0},... | collective-permute-start | bytes 18874376 | tf_op jit(solution)/shard_map/ppermute | solution.py:21
  329.3 283.8 %copy-start.1 = (f32[4,12,32,512]{3,2,1,0:T(8,128)S(1)}, f32[4,12,32,512]{3,2,1,0:T(8,128)}, u32[]{:S(2)}) copy-start(f32[4,12,32,512]{3,2,1,0:T(8,128)} %copy-done) | copy-start | bytes 9437188
  615.1 7.8 copy-start.5
  663.4 63.3 %copy-start.7 = (f32[12,32,512]{2,1,0:T(8,128)S(1)}, f32[12,32,512]{2,1,0:T(8,128)}, u32[]{:S(2)}) copy-start(f32[12,32,512]{2,1,0:T(8,128)} %param.14) | copy-start | bytes 2359300
  755.6 12.5 %copy-start.6 = (f32[12,128,128]{2,1,0:T(8,128)S(1)}, f32[12,128,128]{2,1,0:T(8,128)}, u32[]{:S(2)}) copy-start(f32[12,128,128]{2,1,0:T(8,128)} %param.17) | copy-start | bytes 2359300
  788.1 9.1 copy-start.8
  893.4 5.9 copy-start.10
  906.9 5.3 copy-start.9
  906.9 41.5 %all-to-all-start.1 = ((bf16[24,32,4,512]{3,1,2,0:T(8,128)(2,1)}), bf16[24,32,4,512]{3,1,2,0:T(8,128)(2,1)}, u32[]{:S(2)}, u32[]{:S(2)}) async-start(bf16[24,32,4,512]{3,1,2,0:T(8,128)(2,1)} %multiply_convert_fusion), calls=%async_computation.1 | async-start | bytes 6291456 | tf_op jit(solution)/shard_map/all_to_all | solution.py:152
  948.4 2.4 copy-start.2
  948.4 2.8 copy-start.3
